TPU v7x, 32 devices: a whole 2x2x4 slice. The times are simulated.
32 devices in a mesh: node: 4 (over y, x), grid: 8 (over z, core).
Axes of the slice: x: 2, y: 2, z: 4, core: 2. Of those that a mesh axis runs over, the one named last changes fastest.
Arguments:
- probes: float32 [1, 48, 192, 256], P(None, 'grid'), may hold values from -6 to 6
- potential: float32 [48, 192, 256], P('grid'), may hold values from -2 to 1
- warm_start: bfloat16 [4, 1, 2, 48, 192, 256], P('node', None, None, 'grid'), may hold values from -0.29882812 to 0.29882812
- shift_points: float32 [4, 2], P('node'), may hold values from -4 to 9, as said below
- quad_weights: float32 [4, 2], P('node'), may hold values from -0.3 to 0.3
Outputs:
- moments: float32 [2, 1, 2, 48, 192, 256], P(None, None, None, 'grid', 'node')
- trace_estimate: float32 [2], replicated
Inputs may be any that keep to these rules, and one draw needn't show every extreme that they name: `shift_points`: column 0 holds real parts in -1 to 9; column 1 holds imaginary parts whose magnitude lies in 1 to 4.
All inputs are finite; a program needn't handle non-finite values.
Results may differ from a plain program's by a relative error of at most 0.0003.
Values may be sent and summed in bfloat16 or wider, within the bound.
A program may use at most 192 MiB of HBM per device.

v0:
```python
import jax
import jax.numpy as jnp
from jax import lax
from jax.sharding import PartitionSpec as P

PROBES = 1
ITERS = 2
MOMENTS = 2
near_weight = 4.0 / 3.0
far_weight = -1.0 / 12.0
self_weight = -7.5


def with_halo(cells, sides, width):
    for axis, dim in sides:
        count = lax.axis_size(axis)
        head = lax.slice_in_dim(cells, 0, width, axis=dim)
        tail = lax.slice_in_dim(cells, cells.shape[dim] - width, cells.shape[dim], axis=dim)
        cells = jnp.concatenate(
            [
                lax.ppermute(tail, axis, [(i, (i + 1) % count) for i in range(count)]),
                cells,
                lax.ppermute(head, axis, [((i + 1) % count, i) for i in range(count)]),
            ],
            axis=dim,
        )
    return cells


def hamiltonian_apply(padded, potential, shift_real, shift_imag):
    middle = padded[:, :, :, 2:-2]
    near_sum = (
        padded[:, :, :, 1:-3]
        + padded[:, :, :, 3:-1]
        + (jnp.roll(middle, 1, 4) + jnp.roll(middle, -1, 4))
        + (jnp.roll(middle, 1, 5) + jnp.roll(middle, -1, 5))
    )
    far_sum = (
        padded[:, :, :, :-4]
        + padded[:, :, :, 4:]
        + (jnp.roll(middle, 2, 4) + jnp.roll(middle, -2, 4))
        + (jnp.roll(middle, 2, 5) + jnp.roll(middle, -2, 5))
    )
    laplacian = near_weight * near_sum + far_weight * far_sum + self_weight * middle
    real_shift = shift_real[:, None, None, None, None]
    imag_shift = shift_imag[:, None, None, None, None]
    real_part = middle[:, :, 0]
    imag_part = middle[:, :, 1]
    result_real = (
        real_shift * real_part
        - imag_shift * imag_part
        + 0.5 * laplacian[:, :, 0]
        - potential * real_part
    )
    result_imag = (
        real_shift * imag_part
        + imag_shift * real_part
        + 0.5 * laplacian[:, :, 1]
        - potential * imag_part
    )
    return jnp.stack([result_real, result_imag], axis=2)


def bilinear(first_vec, second_vec):
    real_sum = jnp.sum(
        first_vec[:, :, 0] * second_vec[:, :, 0] - first_vec[:, :, 1] * second_vec[:, :, 1],
        axis=(2, 3, 4),
    )
    imag_sum = jnp.sum(
        first_vec[:, :, 0] * second_vec[:, :, 1] + first_vec[:, :, 1] * second_vec[:, :, 0],
        axis=(2, 3, 4),
    )
    return jnp.stack([real_sum, imag_sum], axis=-1)


def complex_times(factor_one, factor_two):
    return jnp.stack(
        [
            factor_one[..., 0] * factor_two[..., 0] - factor_one[..., 1] * factor_two[..., 1],
            factor_one[..., 0] * factor_two[..., 1] + factor_one[..., 1] * factor_two[..., 0],
        ],
        axis=-1,
    )


def complex_divide(factor_one, factor_two):
    magnitude = factor_two[..., 0] * factor_two[..., 0] + factor_two[..., 1] * factor_two[..., 1]
    return jnp.stack(
        [
            (factor_one[..., 0] * factor_two[..., 0] + factor_one[..., 1] * factor_two[..., 1])
            / magnitude,
            (factor_one[..., 1] * factor_two[..., 0] - factor_one[..., 0] * factor_two[..., 1])
            / magnitude,
        ],
        axis=-1,
    )


def scale_field(scalars, vector):
    real_scalar = scalars[..., 0][:, :, None, None, None]
    imag_scalar = scalars[..., 1][:, :, None, None, None]
    return jnp.stack(
        [
            real_scalar * vector[:, :, 0] - imag_scalar * vector[:, :, 1],
            real_scalar * vector[:, :, 1] + imag_scalar * vector[:, :, 0],
        ],
        axis=2,
    )


def trim_planes(vector, extent_now, extent_out, along_dim):
    excess = extent_now - extent_out
    if excess == 0:
        return vector
    return lax.slice_in_dim(vector, excess, vector.shape[along_dim] - excess, axis=along_dim)


def center(vector, extent):
    return trim_planes(vector, extent, 0, 3)


def residual_norms(vector):
    return lax.psum(bilinear(vector, vector), "grid")


def per_device(probes, potential, warm_start, shift_points, quad_weights):
    shift_real = shift_points[:, 0]
    shift_imag = shift_points[:, 1]
    start_width = 2
    start_wide = with_halo(warm_start, (("grid", 3),), start_width).astype(jnp.float32)
    start_extent = start_width - 2
    solution = warm_start.astype(jnp.float32)
    potential_extent = 0
    source = jnp.stack([probes, jnp.zeros_like(probes)], axis=1)[None]
    residual = source - hamiltonian_apply(
        start_wide,
        trim_planes(potential, potential_extent, start_extent, 0),
        shift_real,
        shift_imag,
    )
    direction = residual
    extent = start_extent
    residual_extent = start_extent
    norm_now = residual_norms(center(residual, start_extent))
    for iteration in range(ITERS):
        padded = with_halo(direction, (("grid", 3),), 2)
        margin = 2
        extent_out = margin - 2
        applied = hamiltonian_apply(
            padded, trim_planes(potential, potential_extent, extent_out, 0), shift_real, shift_imag
        )
        applied, direction, extent = (
            applied,
            trim_planes(padded, margin, extent_out, 3),
            extent_out,
        )
        if iteration == 0:
            residual = direction
            residual_extent = extent
        center_part = center(direction, extent)
        curvature = lax.psum(bilinear(center_part, center(applied, extent)), "grid")
        step_length = complex_divide(norm_now, curvature)
        solution = solution + scale_field(step_length, center_part)
        residual = trim_planes(residual, residual_extent, extent, 3) - scale_field(
            step_length, applied
        )
        residual_extent = extent
        if iteration + 1 < ITERS:
            norm_next = residual_norms(center(residual, extent))
            direction = residual + scale_field(complex_divide(norm_next, norm_now), direction)
            norm_now = norm_next
    scaled_shift = jnp.stack([(shift_real - 4.0) / 5.0, shift_imag / 5.0], axis=-1)
    weight_power = quad_weights
    powers = []
    for degree in range(MOMENTS):
        powers.append(weight_power)
        weight_power = complex_times(weight_power, scaled_shift)
    coefficients = jnp.stack(powers)
    coef_real = coefficients[..., 0]
    coef_imag = coefficients[..., 1]
    highest = lax.Precision.HIGHEST
    sol_real = solution[:, :, 0]
    sol_imag = solution[:, :, 1]
    term_real = jnp.einsum("ks,spzxy->kpzxy", coef_real, sol_real, precision=highest) - jnp.einsum(
        "ks,spzxy->kpzxy", coef_imag, sol_imag, precision=highest
    )
    term_imag = jnp.einsum("ks,spzxy->kpzxy", coef_real, sol_imag, precision=highest) + jnp.einsum(
        "ks,spzxy->kpzxy", coef_imag, sol_real, precision=highest
    )
    moment_terms = jnp.stack([term_real, term_imag], axis=2)
    moments = lax.psum_scatter(moment_terms, "node", scatter_dimension=4, tiled=True)
    inner_sums = jnp.einsum("pzxy,spczxy->sc", probes, solution, precision=highest) / PROBES
    local_trace = jnp.sum(complex_times(quad_weights, inner_sums), axis=0)
    trace_estimate = lax.psum(local_trace, ("node", "grid"))
    return (moments, trace_estimate)


def solution(mesh):
    return jax.shard_map(
        per_device,
        mesh=mesh,
        in_specs=(
            P(None, "grid", None, None),
            P("grid", None, None),
            P("node", None, None, "grid", None, None),
            P("node", None),
            P("node", None),
        ),
        out_specs=(P(None, None, None, "grid", "node", None), P()),
        check_vma=False,
    )
```

profile of v0, /device:TPU:12, one launch (start us, length us, event | category | flops | bytes accessed | tf_op | source)
XLA Modules:
  0.0 308.9 jit_solution(7874606106377025501)
XLA Ops:
  7.2 1.3 fusion.100
  9.0 1.4 fusion.107
  11.8 1.3 fusion.102
  15.6 2.4 collective-permute-done
  18.8 2.2 fusion.79
  21.0 1.4 fusion.80
  22.4 2.6 fusion.78
  25.0 2.9 fusion.76
  27.9 1.8 fusion.77
  29.8 8.3 %fusion.24 = f32[1,1,2,6,192,256]{5,4,3,2,1,0:T(8,128)} fusion(f32[1,1,2,10,192,256]{5,4,3,2,1,0:T(8,128)S(1)} %maximum_convert_fusion, f32[1,1,2,6,191,256]{5,4,3,2,1,0:T(8,128)S(1)} %get-tuple-element.31, f32[1,1,2,6,1,256]{5,4,3,2,1,0:T(1,128)S(1)} %get-tuple-element.83, f32[1,1,2,6,1,256]{5,4,3,2,1,0:T(1,128)S(1)} %get-tuple-element.82, ...), kind=kLoop, calls=%fused_computation.38 | loop fusion | flops 13565952 | bytes 33030144 | tf_op jit(solution)/shard_map/add | solution.py:44
  38.1 3.6 %fusion.54 = (f32[1,1,1,6,192,256]{5,4,3,2,1,0:T(8,128)S(1)}, f32[1,1,1,6,192,256]{5,4,3,2,1,0:T(8,128)S(1)}) fusion(f32[1,1,2,6,192,256]{5,4,3,2,1,0:T(8,128)} %fusion.24, f32[6,192,256]{2,1,0:T(8,128)S(1)} %copy-done.7, f32[1,1,2,10,192,256]{5,4,3,2,1,0:T(8,128)S(1)} %maximum_convert_fusion, f32[]{:T(128)} %bitcast.6, f32[]{:T(128)} %bitcast.4), kind=kLoop, calls=%fused_computation.97 | loop fusion | flops 4128768 | bytes 8257544 | tf_op jit(solution)/shard_map/stack | solution.py:61
  43.2 1.8 fusion.97
  45.0 3.0 fusion.95
  48.0 1.4 fusion.96
  49.5 1.8 fusion.92
  52.8 1.9 pad_maximum_fusion.6
  54.7 2.6 fusion.93
  57.3 2.9 fusion.91
  60.2 3.1 %collective-permute-done.3 = f32[1,1,2,2,192,256]{5,4,3,2,1,0:T(8,128)S(1)} collective-permute-done((f32[1,1,2,2,192,256]{5,4,3,2,1,0:T(8,128)S(1)}, f32[1,1,2,2,192,256]{5,4,3,2,1,0:T(8,128)S(1)}, u32[]{:S(2)}, u32[]{:S(2)}) %collective-permute-start.3) | collective-permute-done | bytes 786464 | tf_op jit(solution)/shard_map/ppermute | solution.py:23
  63.3 10.7 %collective-permute-done.2 = f32[1,1,2,2,192,256]{5,4,3,2,1,0:T(8,128)S(1)} collective-permute-done((f32[1,1,2,2,192,256]{5,4,3,2,1,0:T(8,128)S(1)}, f32[1,1,2,2,192,256]{5,4,3,2,1,0:T(8,128)S(1)}, u32[]{:S(2)}, u32[]{:S(2)}) %collective-permute-start.2) | collective-permute-done | bytes 786464 | tf_op jit(solution)/shard_map/ppermute | solution.py:21
  74.9 9.1 %fusion.14 = f32[1,1,2,6,192,256]{5,4,3,2,1,0:T(8,128)S(1)} fusion(f32[1,1,2,6,192,256]{5,4,3,2,1,0:T(8,128)S(1)} %maximum_subtract_fusion, f32[1,1,2,2,192,256]{5,4,3,2,1,0:T(8,128)} %copy-done.23, f32[1,1,2,2,192,256]{5,4,3,2,1,0:T(8,128)} %copy-done.24, f32[1,1,2,6,191,256]{5,4,3,2,1,0:T(8,128)} %get-tuple-element.75, ...), kind=kLoop, calls=%fused_computation.23 | loop fusion | flops 15925248 | bytes 25165824 | tf_op jit(solution)/shard_map/add | solution.py:44
  84.0 4.3 %fusion.64 = (f32[]{:T(128)}, f32[]{:T(128)}, f32[6,192,256]{2,1,0:T(8,128)}, f32[6,192,256]{2,1,0:T(8,128)}) fusion(f32[1,1,2,6,192,256]{5,4,3,2,1,0:T(8,128)S(1)} %maximum_subtract_fusion, f32[6,192,256]{2,1,0:T(8,128)S(1)} %copy-done.7, f32[1,1,2,6,192,256]{5,4,3,2,1,0:T(8,128)S(1)} %fusion.14, f32[]{:T(128)} %bitcast.6, f32[]{:T(128)} %bitcast.4), kind=kLoop, calls=%fused_computation.124 | loop fusion | flops 6488062 | bytes 8257552 | tf_op jit(solution)/shard_map/reduce_sum | solution.py:65
  88.3 1.8 pad_maximum_fusion.7
  90.2 14.2 %all-reduce.1 = (f32[1,1,2]{2,1,0:T(1,128)S(1)}, f32[1,1,2]{2,1,0:T(1,128)S(1)}) all-reduce(f32[1,1,2]{2,1,0:T(1,128)S(1)} %copy-done.28, f32[1,1,2]{2,1,0:T(1,128)} %pad_maximum_fusion.7), channel_id=1, replica_groups=mesh['node'=4,'grid'=8] {'grid'}, use_global_device_ids=true, to_apply=%region_2.3 | all-reduce | flops 4 | bytes 32 | tf_op jit(solution)/shard_map/psum | solution.py:123
  114.1 2.1 subtract_bitcast_fusion.1
  117.9 1.0 subtract_reduce_fusion
  118.8 1.3 pad_maximum_fusion.8
  121.4 13.6 %psum.37 = f32[1,1,2]{2,1,0:T(1,128)S(1)} all-reduce(f32[1,1,2]{2,1,0:T(1,128)S(1)} %pad_maximum_fusion.8), channel_id=1, replica_groups=mesh['node'=4,'grid'=8] {'grid'}, use_global_device_ids=true, to_apply=%region_8.9 | all-reduce | flops 2 | bytes 16 | tf_op jit(solution)/shard_map/psum | solution.py:123
  141.0 1.9 multiply_subtract_fusion.1
  145.6 3.0 fusion.86
  148.6 1.4 fusion.87
  150.0 1.8 fusion.83
  151.9 3.6 %collective-permute-start.5 = (f32[1,1,2,2,192,256]{5,4,3,2,1,0:T(8,128)S(1)}, f32[1,1,2,2,192,256]{5,4,3,2,1,0:T(8,128)S(1)}, u32[]{:S(2)}, u32[]{:S(2)}) collective-permute-start(f32[1,1,2,2,192,256]{5,4,3,2,1,0:T(8,128)S(1)} %get-tuple-element.55), channel_id=1, source_target_pairs={{1,0},{2,1},{3,2},{4,3},{5,4},{6,5},{7,6},{0,7},{9,8},{10,9},{11,1... | collective-permute-start | bytes 2359304 | tf_op jit(solution)/shard_map/ppermute | solution.py:23
  155.4 2.6 fusion.84
  158.1 2.9 fusion.82
  161.0 12.4 %collective-permute-done.5 = f32[1,1,2,2,192,256]{5,4,3,2,1,0:T(8,128)S(1)} collective-permute-done((f32[1,1,2,2,192,256]{5,4,3,2,1,0:T(8,128)S(1)}, f32[1,1,2,2,192,256]{5,4,3,2,1,0:T(8,128)S(1)}, u32[]{:S(2)}, u32[]{:S(2)}) %collective-permute-start.5) | collective-permute-done | bytes 786464 | tf_op jit(solution)/shard_map/ppermute | solution.py:23
  175.3 9.9 %fusion.6 = f32[1,1,2,6,192,256]{5,4,3,2,1,0:T(8,128)} fusion(f32[1,1,2,6,192,256]{5,4,3,2,1,0:T(8,128)S(1)} %maximum_add_fusion.9, f32[1,1,2,2,192,256]{5,4,3,2,1,0:T(8,128)} %copy-done.25, f32[1,1,2,2,192,256]{5,4,3,2,1,0:T(8,128)} %copy-done.26, f32[1,1,2,6,191,256]{5,4,3,2,1,0:T(8,128)S(1)} %get-tuple-element.51, ...), kind=kLoop, calls=%fused_computation.15 | loop fusion | flops 15925248 | bytes 25165824 | tf_op jit(solution)/shard_map/add | solution.py:44
  185.2 3.5 %fusion.40 = (f32[6,192,256]{2,1,0:T(8,128)S(1)}, f32[6,192,256]{2,1,0:T(8,128)S(1)}) fusion(f32[1,1,2,6,192,256]{5,4,3,2,1,0:T(8,128)} %fusion.6, f32[6,192,256]{2,1,0:T(8,128)S(1)} %copy-done.8, f32[1,1,2,6,192,256]{5,4,3,2,1,0:T(8,128)S(1)} %maximum_add_fusion.9, f32[]{:T(128)} %bitcast.6, f32[]{:T(128)} %bitcast.4), kind=kLoop, calls=%fused_computation.79 | loop fusion | flops 4128768 | bytes 8257544 | tf_op jit(solution)/shard_map/sub | solution.py:50
  188.7 1.2 fusion.58
  189.9 2.0 pad_maximum_fusion.9
  192.1 12.2 %psum.38 = f32[1,1,2]{2,1,0:T(1,128)S(1)} all-reduce(f32[1,1,2]{2,1,0:T(1,128)} %pad_maximum_fusion.9), channel_id=1, replica_groups=mesh['node'=4,'grid'=8] {'grid'}, use_global_device_ids=true, to_apply=%region_11.12 | all-reduce | flops 2 | bytes 16 | tf_op jit(solution)/shard_map/psum | solution.py:161
  213.1 1.0 copy-done.21
  214.1 1.2 copy-done.22
  216.5 2.6 pad_maximum_fusion
  219.2 1.2 copy-done.14
  220.8 2.1 fusion.108
  222.9 29.6 %fusion.68 = f32[1,2]{1,0:T(1,128)S(1)} fusion(f32[6,192,256,1]{2,1,0,3:T(8,128)S(1)} %bitcast.197, f32[2,6,192,256]{3,2,1,0:T(8,128)S(1)} %fusion.108), kind=kOutput, calls=%fused_computation.145 | convolution fusion | flops 7077888 | bytes 3538952 | tf_op jit(solution)/shard_map/pzxy,spczxy->sc/dot_general | solution.py:192
  258.1 44.0 %psum.39 = f32[2]{0:T(128)} all-reduce(f32[2]{0:T(128)S(1)} %maximum_bitcast_fusion.1), channel_id=1, replica_groups=mesh['node'=4,'grid'=8] {'node','grid'}, use_global_device_ids=true, to_apply=%region_13.14 | all-reduce | flops 2 | bytes 16 | tf_op jit(solution)/shard_map/psum | solution.py:194
  (91 shorter events, 16.3 us)
Async XLA Ops:
  7.2 10.8 %copy-start = (bf16[1,1,2,6,192,256]{5,4,3,2,1,0:T(8,128)(2,1)S(1)}, bf16[1,1,2,6,192,256]{5,4,3,2,1,0:T(8,128)(2,1)}, u32[]{:S(2)}) copy-start(bf16[1,1,2,6,192,256]{5,4,3,2,1,0:T(8,128)(2,1)} %param.7) | copy-start | bytes 3538948
  7.2 294.9 %reduce-scatter.2.cloned.1.call-start = ((), (), s32[]{:S(2)}) async-start(), calls=%async_computation.1 | async-start | bytes 5898240 | tf_op jit(solution)/shard_map/reduce_scatter | solution.py:191
  8.5 7.1 %collective-permute-start.1 = (bf16[1,1,2,2,192,256]{5,4,3,2,1,0:T(8,128)(2,1)S(1)}, bf16[1,1,2,2,192,256]{5,4,3,2,1,0:T(8,128)(2,1)S(1)}, u32[]{:S(2)}, u32[]{:S(2)}) collective-permute-start(bf16[1,1,2,2,192,256]{5,4,3,2,1,0:T(8,128)(2,1)S(1)} %get-tuple-element.85), channel_id=1, source_target_pairs={{1,0},{2,1},{3,2},{4,3},{5,4},{6,5},{7,6},{0,7},{9,8},{10,9},{11,1... | collective-permute-start | bytes 1179656 | tf_op jit(solution)/shard_map/ppermute | solution.py:23
  8.5 9.4 %collective-permute-start = (bf16[1,1,2,2,192,256]{5,4,3,2,1,0:T(8,128)(2,1)S(1)}, bf16[1,1,2,2,192,256]{5,4,3,2,1,0:T(8,128)(2,1)S(1)}, u32[]{:S(2)}, u32[]{:S(2)}) collective-permute-start(bf16[1,1,2,2,192,256]{5,4,3,2,1,0:T(8,128)(2,1)S(1)} %get-tuple-element.84), channel_id=1, source_target_pairs={{0,1},{1,2},{2,3},{3,4},{4,5},{5,6},{6,7},{7,0},{8,9},{9,10},{10,1... | collective-permute-start | bytes 1179656 | tf_op jit(solution)/shard_map/ppermute | solution.py:21
  29.8 8.3 %copy-start.7 = (f32[6,192,256]{2,1,0:T(8,128)S(1)}, f32[6,192,256]{2,1,0:T(8,128)}, u32[]{:S(2)}) copy-start(f32[6,192,256]{2,1,0:T(8,128)} %param.6) | copy-start | bytes 3538948
  38.1 3.6 %copy-start.17 = (f32[1,6,192,256]{3,2,1,0:T(8,128)S(1)}, f32[1,6,192,256]{3,2,1,0:T(8,128)}, u32[]{:S(2)}) copy-start(f32[1,6,192,256]{3,2,1,0:T(8,128)} %param.5) | copy-start | bytes 3538948
  41.7 1.0 copy-start.1
  41.7 1.4 copy-start.4
  52.3 11.0 %collective-permute-start.3 = (f32[1,1,2,2,192,256]{5,4,3,2,1,0:T(8,128)S(1)}, f32[1,1,2,2,192,256]{5,4,3,2,1,0:T(8,128)S(1)}, u32[]{:S(2)}, u32[]{:S(2)}) collective-permute-start(f32[1,1,2,2,192,256]{5,4,3,2,1,0:T(8,128)S(1)} %get-tuple-element.79), channel_id=1, source_target_pairs={{1,0},{2,1},{3,2},{4,3},{5,4},{6,5},{7,6},{0,7},{9,8},{10,9},{11,1... | collective-permute-start | bytes 2359304 | tf_op jit(solution)/shard_map/ppermute | solution.py:23
  52.3 21.7 %collective-permute-start.2 = (f32[1,1,2,2,192,256]{5,4,3,2,1,0:T(8,128)S(1)}, f32[1,1,2,2,192,256]{5,4,3,2,1,0:T(8,128)S(1)}, u32[]{:S(2)}, u32[]{:S(2)}) collective-permute-start(f32[1,1,2,2,192,256]{5,4,3,2,1,0:T(8,128)S(1)} %get-tuple-element.78), channel_id=1, source_target_pairs={{0,1},{1,2},{2,3},{3,4},{4,5},{5,6},{6,7},{7,0},{8,9},{9,10},{10,1... | collective-permute-start | bytes 2359304 | tf_op jit(solution)/shard_map/ppermute | solution.py:21
  63.3 10.7 %copy-start.23 = (f32[1,1,2,2,192,256]{5,4,3,2,1,0:T(8,128)}, f32[1,1,2,2,192,256]{5,4,3,2,1,0:T(8,128)S(1)}, u32[]{:S(2)}) copy-start(f32[1,1,2,2,192,256]{5,4,3,2,1,0:T(8,128)S(1)} %collective-permute-done.3) | copy-start | bytes 2359300
  74.0 0.9 copy-start.24
  84.0 6.2 %copy-start.28 = (f32[1,1,2]{2,1,0:T(1,128)S(1)}, f32[1,1,2]{2,1,0:T(1,128)}, u32[]{:S(2)}) copy-start(f32[1,1,2]{2,1,0:T(1,128)} %pad_maximum_fusion.6) | copy-start | bytes 28
  114.1 2.2 copy-start.2
  114.1 2.3 copy-start.5
  114.1 2.7 copy-start.18
  116.3 1.0 copy-start.9
  116.3 1.6 copy-start.11
  140.9 2.0 copy-start.3
  140.9 2.0 copy-start.6
  140.9 2.8 copy-start.10
  141.0 3.2 %copy-start.12 = (f32[1,1,1,6,192,256]{5,4,3,2,1,0:T(8,128)S(1)}, f32[1,1,1,6,192,256]{5,4,3,2,1,0:T(8,128)}, u32[]{:S(2)}) copy-start(f32[1,1,1,6,192,256]{5,4,3,2,1,0:T(8,128)} %copy-done.11) | copy-start | bytes 3538948
  141.0 3.5 %copy-start.19 = (f32[1,6,192,256]{3,2,1,0:T(8,128)S(1)}, f32[1,6,192,256]{3,2,1,0:T(8,128)}, u32[]{:S(2)}) copy-start(f32[1,6,192,256]{3,2,1,0:T(8,128)} %param.5) | copy-start | bytes 3538948
  151.9 21.5 %collective-permute-start.5 = (f32[1,1,2,2,192,256]{5,4,3,2,1,0:T(8,128)S(1)}, f32[1,1,2,2,192,256]{5,4,3,2,1,0:T(8,128)S(1)}, u32[]{:S(2)}, u32[]{:S(2)}) collective-permute-start(f32[1,1,2,2,192,256]{5,4,3,2,1,0:T(8,128)S(1)} %get-tuple-element.55), channel_id=1, source_target_pairs={{1,0},{2,1},{3,2},{4,3},{5,4},{6,5},{7,6},{0,7},{9,8},{10,9},{11,1... | collective-permute-start | bytes 2359304 | tf_op jit(solution)/shard_map/ppermute | solution.py:23
  155.4 18.9 %collective-permute-start.4 = (f32[1,1,2,2,192,256]{5,4,3,2,1,0:T(8,128)S(1)}, f32[1,1,2,2,192,256]{5,4,3,2,1,0:T(8,128)S(1)}, u32[]{:S(2)}, u32[]{:S(2)}) collective-permute-start(f32[1,1,2,2,192,256]{5,4,3,2,1,0:T(8,128)S(1)} %get-tuple-element.54), channel_id=1, source_target_pairs={{0,1},{1,2},{2,3},{3,4},{4,5},{5,6},{6,7},{7,0},{8,9},{9,10},{10,1... | collective-permute-start | bytes 2359304 | tf_op jit(solution)/shard_map/ppermute | solution.py:21
  173.4 1.0 copy-start.25
  174.4 0.9 copy-start.26
  175.3 9.9 %copy-start.8 = (f32[6,192,256]{2,1,0:T(8,128)S(1)}, f32[6,192,256]{2,1,0:T(8,128)}, u32[]{:S(2)}) copy-start(f32[6,192,256]{2,1,0:T(8,128)} %param.6) | copy-start | bytes 3538948
  188.7 3.2 %copy-start.27 = (f32[1,2]{1,0:T(1,128)S(1)}, f32[1,2]{1,0:T(1,128)}, u32[]{:S(2)}) copy-start(f32[1,2]{1,0:T(1,128)} %param.9) | copy-start | bytes 28
  212.8 1.3 copy-start.21
  212.8 2.5 copy-start.22
  213.1 2.6 copy-start.13
  213.1 2.6 copy-start.15
  219.1 1.3 copy-start.14
  219.1 1.6 copy-start.16
  220.8 2.1 copy-start.20
Sparse Core Ops, SparseCore 0:
  219.3 59.3 reduce-scatter.1
where the time goes:
time: 310 us; the launch traced here: 309 us
  blocking collectives  84 us (27%)
  other arithmetic  60.8 us (20%)
  local copies, waits for them, and re-layouts  53.7 us (17%)
  between operations  46.6 us (15%)
  matrix products  29.6 us (10%)
  waiting for transfers between devices  29.5 us (10%)
  starting transfers between devices  4.66 us (2%)
    psum x1, blocking collectives, per_device(): trace_estimate = lax.psum(local_trace, ('node', 'grid'))  44 us
    dot_general x1, matrix products, per_device(): jnp.einsum('pzxy,spczxy->sc', probes, solution, precision=highest) / PROBES  29.6 us
    psum x2, blocking collectives, residual_norms(): return lax.psum(bilinear(vector, vector), 'grid')  27.8 us
    add x3, other arithmetic, hamiltonian_apply(): near_weight * near_sum + far_weight * far_sum + self_weight * middle  27.3 us
    ppermute x3, waiting for transfers between devices, with_halo(): lax.ppermute(head, axis, [((i + 1) % count, i) for i in range(count)])  15.5 us
    slice x6, local copies, waits for them, and re-layouts, hamiltonian_apply(): jnp.roll(middle, -2, 5)  14.3 us
    ppermute x3, waiting for transfers between devices, with_halo(): lax.ppermute(tail, axis, [(i, (i + 1) % count) for i in range(count)])  14 us
    slice x6, local copies, waits for them, and re-layouts, hamiltonian_apply(): jnp.roll(middle, -1, 5)  12.4 us
  transfers between devices with their start and end apart: 7, of which 5 were waited for; matrix products, arithmetic and copies ran while one was open for 16% of the time, Pallas kernels for 0%

commit v1 on v0

--- a/solution.py
+++ b/solution.py
@@ -158,7 +158,9 @@
             residual = direction
             residual_extent = extent
         center_part = center(direction, extent)
-        curvature = lax.psum(bilinear(center_part, center(applied, extent)), "grid")
+        curvature = jnp.sum(
+            lax.all_gather(bilinear(center_part, center(applied, extent)), "grid"), axis=0
+        )
         step_length = complex_divide(norm_now, curvature)
         solution = solution + scale_field(step_length, center_part)
         residual = trim_planes(residual, residual_extent, extent, 3) - scale_field(

time: 310 us -> 324 us (1.045)
  blocking collectives: 84 us -> 101 us
  other arithmetic: 60.8 us -> 57.3 us
    all_gather x0 -> x2, blocking collectives: none -> 20.7 us  [per_device(): lax.all_gather(bilinear(center_part, center(applied, extent)), 'grid')]
    psum x1 -> x0, blocking collectives: 12.2 us -> none  [per_device(): curvature = lax.psum(bilinear(center_part, center(applied, extent)), 'grid')]
    psum x2, blocking collectives: 27.8 us -> 38.7 us  [residual_norms(): return lax.psum(bilinear(vector, vector), 'grid')]
    reduce_scatter x1, waiting for transfers between devices: 0.01 us -> 10.8 us  [per_device(): lax.psum_scatter(moment_terms, 'node', scatter_dimension=4, tiled=True)]
    ppermute x3, waiting for transfers between devices: 14 us -> 6.66 us  [with_halo(): lax.ppermute(tail, axis, [(i, (i + 1) % count) for i in range(count)])]
    unnamed x58 -> x54, local copies, waits for them, and re-layouts: 9.48 us -> 6.86 us
  transfers between devices with their start and end apart: 7 -> 7, of which waited for: 5 -> 5; matrix products, arithmetic and copies ran while one was open for 16% -> 5% of each run, Pallas kernels for 0% -> 0%
where the time goes in v1:
time: 324 us; the launch traced here: 321 us
  blocking collectives  101 us (31%)
  other arithmetic  57.3 us (18%)
  local copies, waits for them, and re-layouts  52.9 us (16%)
  between operations  45.2 us (14%)
  waiting for transfers between devices  32.1 us (10%)
  matrix products  29.5 us (9%)
    psum x1, blocking collectives, per_device(): trace_estimate = lax.psum(local_trace, ('node', 'grid'))  42 us
    psum x2, blocking collectives, residual_norms(): return lax.psum(bilinear(vector, vector), 'grid')  38.7 us
    dot_general x1, matrix products, per_device(): jnp.einsum('pzxy,spczxy->sc', probes, solution, precision=highest) / PROBES  29.5 us
    add x3, other arithmetic, hamiltonian_apply(): near_weight * near_sum + far_weight * far_sum + self_weight * middle  26.6 us
    all_gather x2, blocking collectives, per_device(): lax.all_gather(bilinear(center_part, center(applied, extent)), 'grid')  20.7 us
    ppermute x3, waiting for transfers between devices, with_halo(): lax.ppermute(head, axis, [((i + 1) % count, i) for i in range(count)])  14.5 us
    slice x6, local copies, waits for them, and re-layouts, hamiltonian_apply(): jnp.roll(middle, -2, 5)  14.2 us
    slice x6, local copies, waits for them, and re-layouts, hamiltonian_apply(): jnp.roll(middle, -1, 5)  11.8 us
  transfers between devices with their start and end apart: 7, of which 5 were waited for; matrix products, arithmetic and copies ran while one was open for 5% of the time, Pallas kernels for 0%

profile of v1, /device:TPU:12, one launch (start us, length us, event | category | flops | bytes accessed | tf_op | source)
XLA Modules:
  0.0 321.1 jit_solution(17876856478569683458)
XLA Ops:
  7.2 1.3 fusion.100
  9.0 1.4 fusion.107
  11.7 2.1 collective-permute-done.1
  13.8 4.1 %collective-permute-done = bf16[1,1,2,2,192,256]{5,4,3,2,1,0:T(8,128)(2,1)S(1)} collective-permute-done((bf16[1,1,2,2,192,256]{5,4,3,2,1,0:T(8,128)(2,1)S(1)}, bf16[1,1,2,2,192,256]{5,4,3,2,1,0:T(8,128)(2,1)S(1)}, u32[]{:S(2)}, u32[]{:S(2)}) %collective-permute-start) | collective-permute-done | bytes 393248 | tf_op jit(solution)/shard_map/ppermute | solution.py:21
  18.8 2.2 fusion.79
  21.4 2.6 fusion.78
  24.0 2.9 fusion.76
  26.9 1.8 fusion.77
  28.8 7.9 %fusion.24 = f32[1,1,2,6,192,256]{5,4,3,2,1,0:T(8,128)} fusion(f32[1,1,2,10,192,256]{5,4,3,2,1,0:T(8,128)S(1)} %maximum_convert_fusion, f32[1,1,2,6,191,256]{5,4,3,2,1,0:T(8,128)S(1)} %get-tuple-element.29, f32[1,1,2,6,1,256]{5,4,3,2,1,0:T(1,128)S(1)} %get-tuple-element.81, f32[1,1,2,6,1,256]{5,4,3,2,1,0:T(1,128)S(1)} %get-tuple-element.80, ...), kind=kLoop, calls=%fused_computation.38 | loop fusion | flops 13565952 | bytes 33030144 | tf_op jit(solution)/shard_map/add | solution.py:44
  36.7 3.5 %fusion.54 = (f32[1,1,1,6,192,256]{5,4,3,2,1,0:T(8,128)S(1)}, f32[1,1,1,6,192,256]{5,4,3,2,1,0:T(8,128)S(1)}) fusion(f32[1,1,2,6,192,256]{5,4,3,2,1,0:T(8,128)} %fusion.24, f32[6,192,256]{2,1,0:T(8,128)S(1)} %copy-done.7, f32[1,1,2,10,192,256]{5,4,3,2,1,0:T(8,128)S(1)} %maximum_convert_fusion, f32[]{:T(128)} %bitcast.6, f32[]{:T(128)} %bitcast.4), kind=kLoop, calls=%fused_computation.97 | loop fusion | flops 4128768 | bytes 8257544 | tf_op jit(solution)/shard_map/stack | solution.py:61
  41.7 1.3 fusion.99
  43.0 2.6 fusion.97
  46.2 3.0 fusion.95
  49.2 1.8 fusion.96
  51.6 1.8 fusion.92
  53.4 1.0 subtract_reduce_fusion.1
  54.5 2.0 pad_maximum_fusion.6
  57.0 27.3 %psum.21 = f32[1,1,2]{2,1,0:T(1,128)S(1)} all-reduce(f32[1,1,2]{2,1,0:T(1,128)} %pad_maximum_fusion.6), channel_id=1, replica_groups=mesh['node'=4,'grid'=8] {'grid'}, use_global_device_ids=true, to_apply=%region_2.3 | all-reduce | flops 2 | bytes 16 | tf_op jit(solution)/shard_map/psum | solution.py:123
  86.2 2.6 fusion.93
  88.9 2.9 fusion.91
  91.9 9.2 %fusion.14 = f32[1,1,2,6,192,256]{5,4,3,2,1,0:T(8,128)S(1)} fusion(f32[1,1,2,6,192,256]{5,4,3,2,1,0:T(8,128)S(1)} %maximum_subtract_fusion, f32[1,1,2,2,192,256]{5,4,3,2,1,0:T(8,128)} %collective-permute-done.3, f32[1,1,2,2,192,256]{5,4,3,2,1,0:T(8,128)} %collective-permute-done.2, f32[1,1,2,6,191,256]{5,4,3,2,1,0:T(8,128)} %get-tuple-element.73, ...), kind=kLoop, calls=%fused_computation.23 | loop fusion | flops 15925248 | bytes 25165824 | tf_op jit(solution)/shard_map/add | solution.py:44
  101.1 4.1 %fusion.64 = (f32[]{:T(128)}, f32[]{:T(128)}, f32[6,192,256]{2,1,0:T(8,128)}, f32[6,192,256]{2,1,0:T(8,128)}) fusion(f32[1,1,2,6,192,256]{5,4,3,2,1,0:T(8,128)S(1)} %maximum_subtract_fusion, f32[6,192,256]{2,1,0:T(8,128)S(1)} %copy-done.8, f32[1,1,2,6,192,256]{5,4,3,2,1,0:T(8,128)S(1)} %fusion.14, f32[]{:T(128)} %bitcast.6, f32[]{:T(128)} %bitcast.4), kind=kLoop, calls=%fused_computation.124 | loop fusion | flops 6488062 | bytes 8257552 | tf_op jit(solution)/shard_map/reduce_sum | solution.py:65
  105.2 1.2 pad_maximum_fusion.7
  107.7 12.4 %all-gather = f32[8,1,2]{2,1,0:T(1,128)S(1)} all-gather(f32[1,1,2]{2,1,0:T(1,128)S(1)} %pad_maximum_fusion.7), channel_id=2, replica_groups=mesh['node'=4,'grid'=8] {'grid'}, dimensions={0}, use_global_device_ids=true | all-gather | bytes 72 | tf_op jit(solution)/shard_map/all_gather | solution.py:162
  127.8 2.1 subtract_bitcast_fusion.1
  131.5 0.9 subtract_reduce_fusion
  132.4 1.3 pad_maximum_fusion.8
  133.7 11.4 %psum.22 = f32[1,1,2]{2,1,0:T(1,128)S(1)} all-reduce(f32[1,1,2]{2,1,0:T(1,128)S(1)} %pad_maximum_fusion.8), channel_id=1, replica_groups=mesh['node'=4,'grid'=8] {'grid'}, use_global_device_ids=true, to_apply=%region_8.9 | all-reduce | flops 2 | bytes 16 | tf_op jit(solution)/shard_map/psum | solution.py:123
  150.7 1.9 multiply_subtract_fusion.1
  155.4 3.0 fusion.86
  158.3 1.4 fusion.87
  159.8 1.8 fusion.83
  161.6 1.6 collective-permute-start.5
  163.2 2.6 fusion.84
  165.9 2.9 fusion.82
  168.8 12.4 %collective-permute-done.5 = f32[1,1,2,2,192,256]{5,4,3,2,1,0:T(8,128)S(1)} collective-permute-done((f32[1,1,2,2,192,256]{5,4,3,2,1,0:T(8,128)S(1)}, f32[1,1,2,2,192,256]{5,4,3,2,1,0:T(8,128)S(1)}, u32[]{:S(2)}, u32[]{:S(2)}) %collective-permute-start.5) | collective-permute-done | bytes 786464 | tf_op jit(solution)/shard_map/ppermute | solution.py:23
  181.2 2.5 collective-permute-done.4
  183.7 0.9 copy-done.22
  184.6 9.5 %fusion.6 = f32[1,1,2,6,192,256]{5,4,3,2,1,0:T(8,128)} fusion(f32[1,1,2,6,192,256]{5,4,3,2,1,0:T(8,128)S(1)} %maximum_add_fusion.9, f32[1,1,2,2,192,256]{5,4,3,2,1,0:T(8,128)S(1)} %collective-permute-done.5, f32[1,1,2,2,192,256]{5,4,3,2,1,0:T(8,128)} %copy-done.22, f32[1,1,2,6,191,256]{5,4,3,2,1,0:T(8,128)S(1)} %get-tuple-element.49, ...), kind=kLoop, calls=%fused_computation.15 | loop fusion | flops 15925248 | bytes 25165824 | tf_op jit(solution)/shard_map/add | solution.py:44
  194.1 3.4 %fusion.40 = (f32[6,192,256]{2,1,0:T(8,128)S(1)}, f32[6,192,256]{2,1,0:T(8,128)S(1)}) fusion(f32[1,1,2,6,192,256]{5,4,3,2,1,0:T(8,128)} %fusion.6, f32[6,192,256]{2,1,0:T(8,128)S(1)} %copy-done.9, f32[1,1,2,6,192,256]{5,4,3,2,1,0:T(8,128)S(1)} %maximum_add_fusion.9, f32[]{:T(128)} %bitcast.6, f32[]{:T(128)} %bitcast.4), kind=kLoop, calls=%fused_computation.79 | loop fusion | flops 4128768 | bytes 8257544 | tf_op jit(solution)/shard_map/sub | solution.py:50
  197.5 1.2 fusion.58
  198.7 1.3 pad_maximum_fusion.9
  200.1 8.3 %all-gather.1 = f32[8,1,2]{2,1,0:T(1,128)S(1)} all-gather(f32[1,1,2]{2,1,0:T(1,128)S(1)} %pad_maximum_fusion.9), channel_id=3, replica_groups=mesh['node'=4,'grid'=8] {'grid'}, dimensions={0}, use_global_device_ids=true | all-gather | bytes 72 | tf_op jit(solution)/shard_map/all_gather | solution.py:162
  217.0 0.9 copy-done.18
  219.9 29.5 %fusion.68 = f32[1,2]{1,0:T(1,128)S(1)} fusion(f32[6,192,256,1]{2,1,0,3:T(8,128)S(1)} %bitcast.199, f32[2,6,192,256]{3,2,1,0:T(8,128)S(1)} %fusion.108), kind=kOutput, calls=%fused_computation.145 | convolution fusion | flops 7077888 | bytes 3538952 | tf_op jit(solution)/shard_map/pzxy,spczxy->sc/dot_general | solution.py:194
  253.7 2.6 pad_maximum_fusion
  261.4 42.0 %psum.23 = f32[2]{0:T(128)} all-reduce(f32[2]{0:T(128)S(1)} %maximum_bitcast_fusion.1), channel_id=1, replica_groups=mesh['node'=4,'grid'=8] {'node','grid'}, use_global_device_ids=true, to_apply=%region_13.14 | all-reduce | flops 2 | bytes 16 | tf_op jit(solution)/shard_map/psum | solution.py:196
  303.4 10.8 %reduce-scatter.2.cloned.1.call-done = f32[2,1,2,6,48,256]{5,4,3,2,1,0:T(8,128)} async-done(((f32[2,1,2,6,192,256]{5,4,3,2,1,0:T(8,128)}), f32[2,1,2,6,48,256]{5,4,3,2,1,0:T(8,128)}) %reduce-scatter.2.cloned.1.call-update) | async-done | bytes 1179664 | tf_op jit(solution)/shard_map/reduce_scatter | solution.py:193
  (90 shorter events, 16.1 us)
Async XLA Ops:
  7.2 10.8 %copy-start = (bf16[1,1,2,6,192,256]{5,4,3,2,1,0:T(8,128)(2,1)S(1)}, bf16[1,1,2,6,192,256]{5,4,3,2,1,0:T(8,128)(2,1)}, u32[]{:S(2)}) copy-start(bf16[1,1,2,6,192,256]{5,4,3,2,1,0:T(8,128)(2,1)} %param.7) | copy-start | bytes 3538948
  7.2 307.0 %reduce-scatter.2.cloned.1.call-start = ((), (), s32[]{:S(2)}) async-start(), calls=%async_computation.1 | async-start | bytes 5898240 | tf_op jit(solution)/shard_map/reduce_scatter | solution.py:193
  8.5 5.4 %collective-permute-start.1 = (bf16[1,1,2,2,192,256]{5,4,3,2,1,0:T(8,128)(2,1)S(1)}, bf16[1,1,2,2,192,256]{5,4,3,2,1,0:T(8,128)(2,1)S(1)}, u32[]{:S(2)}, u32[]{:S(2)}) collective-permute-start(bf16[1,1,2,2,192,256]{5,4,3,2,1,0:T(8,128)(2,1)S(1)} %get-tuple-element.83), channel_id=1, source_target_pairs={{1,0},{2,1},{3,2},{4,3},{5,4},{6,5},{7,6},{0,7},{9,8},{10,9},{11,1... | collective-permute-start | bytes 1179656 | tf_op jit(solution)/shard_map/ppermute | solution.py:23
  8.5 9.4 %collective-permute-start = (bf16[1,1,2,2,192,256]{5,4,3,2,1,0:T(8,128)(2,1)S(1)}, bf16[1,1,2,2,192,256]{5,4,3,2,1,0:T(8,128)(2,1)S(1)}, u32[]{:S(2)}, u32[]{:S(2)}) collective-permute-start(bf16[1,1,2,2,192,256]{5,4,3,2,1,0:T(8,128)(2,1)S(1)} %get-tuple-element.82), channel_id=1, source_target_pairs={{0,1},{1,2},{2,3},{3,4},{4,5},{5,6},{6,7},{7,0},{8,9},{9,10},{10,1... | collective-permute-start | bytes 1179656 | tf_op jit(solution)/shard_map/ppermute | solution.py:21
  28.8 8.0 %copy-start.7 = (f32[6,192,256]{2,1,0:T(8,128)S(1)}, f32[6,192,256]{2,1,0:T(8,128)}, u32[]{:S(2)}) copy-start(f32[6,192,256]{2,1,0:T(8,128)} %param.6) | copy-start | bytes 3538948
  36.7 3.6 %copy-start.14 = (f32[1,6,192,256]{3,2,1,0:T(8,128)S(1)}, f32[1,6,192,256]{3,2,1,0:T(8,128)}, u32[]{:S(2)}) copy-start(f32[1,6,192,256]{3,2,1,0:T(8,128)} %param.5) | copy-start | bytes 3538948
  40.3 1.1 copy-start.1
  40.3 1.4 copy-start.4
  54.5 37.3 %collective-permute-start.3 = (f32[1,1,2,2,192,256]{5,4,3,2,1,0:T(8,128)}, f32[1,1,2,2,192,256]{5,4,3,2,1,0:T(8,128)}, u32[]{:S(2)}, u32[]{:S(2)}) collective-permute-start(f32[1,1,2,2,192,256]{5,4,3,2,1,0:T(8,128)} %get-tuple-element.77), channel_id=1, source_target_pairs={{1,0},{2,1},{3,2},{4,3},{5,4},{6,5},{7,6},{0,7},{9,8},{10,9},{11,1... | collective-permute-start | bytes 2359304 | tf_op jit(solution)/shard_map/ppermute | solution.py:23
  56.5 35.3 %collective-permute-start.2 = (f32[1,1,2,2,192,256]{5,4,3,2,1,0:T(8,128)}, f32[1,1,2,2,192,256]{5,4,3,2,1,0:T(8,128)}, u32[]{:S(2)}, u32[]{:S(2)}) collective-permute-start(f32[1,1,2,2,192,256]{5,4,3,2,1,0:T(8,128)} %get-tuple-element.76), channel_id=1, source_target_pairs={{0,1},{1,2},{2,3},{3,4},{4,5},{5,6},{6,7},{7,0},{8,9},{9,10},{10,1... | collective-permute-start | bytes 2359304 | tf_op jit(solution)/shard_map/ppermute | solution.py:21
  88.8 3.0 copy-start.20
  88.8 3.0 copy-start.21
  88.8 3.0 copy-start.23
  88.9 3.0 copy-start.24
  88.9 3.0 copy-start.25
  91.9 9.2 %copy-start.8 = (f32[6,192,256]{2,1,0:T(8,128)S(1)}, f32[6,192,256]{2,1,0:T(8,128)}, u32[]{:S(2)}) copy-start(f32[6,192,256]{2,1,0:T(8,128)} %param.6) | copy-start | bytes 3538948
  127.7 2.2 copy-start.2
  127.7 2.3 copy-start.5
  127.8 2.7 copy-start.15
  129.9 1.0 copy-start.10
  129.9 1.6 copy-start.12
  150.7 2.0 copy-start.3
  150.7 2.0 copy-start.6
  150.7 2.8 copy-start.11
  150.7 3.2 copy-start.13
  150.7 3.5 %copy-start.16 = (f32[1,6,192,256]{3,2,1,0:T(8,128)S(1)}, f32[1,6,192,256]{3,2,1,0:T(8,128)}, u32[]{:S(2)}) copy-start(f32[1,6,192,256]{3,2,1,0:T(8,128)} %param.5) | copy-start | bytes 3538948
  161.6 19.6 %collective-permute-start.5 = (f32[1,1,2,2,192,256]{5,4,3,2,1,0:T(8,128)S(1)}, f32[1,1,2,2,192,256]{5,4,3,2,1,0:T(8,128)S(1)}, u32[]{:S(2)}, u32[]{:S(2)}) collective-permute-start(f32[1,1,2,2,192,256]{5,4,3,2,1,0:T(8,128)S(1)} %get-tuple-element.53), channel_id=1, source_target_pairs={{1,0},{2,1},{3,2},{4,3},{5,4},{6,5},{7,6},{0,7},{9,8},{10,9},{11,1... | collective-permute-start | bytes 2359304 | tf_op jit(solution)/shard_map/ppermute | solution.py:23
  163.2 20.5 %collective-permute-start.4 = (f32[1,1,2,2,192,256]{5,4,3,2,1,0:T(8,128)S(1)}, f32[1,1,2,2,192,256]{5,4,3,2,1,0:T(8,128)S(1)}, u32[]{:S(2)}, u32[]{:S(2)}) collective-permute-start(f32[1,1,2,2,192,256]{5,4,3,2,1,0:T(8,128)S(1)} %get-tuple-element.52), channel_id=1, source_target_pairs={{0,1},{1,2},{2,3},{3,4},{4,5},{5,6},{6,7},{7,0},{8,9},{9,10},{10,1... | collective-permute-start | bytes 2359304 | tf_op jit(solution)/shard_map/ppermute | solution.py:21
  183.7 0.9 copy-start.22
  184.6 9.5 %copy-start.9 = (f32[6,192,256]{2,1,0:T(8,128)S(1)}, f32[6,192,256]{2,1,0:T(8,128)}, u32[]{:S(2)}) copy-start(f32[6,192,256]{2,1,0:T(8,128)} %param.6) | copy-start | bytes 3538948
  216.6 1.3 copy-start.18
  216.6 1.6 copy-start.19
  218.7 1.3 copy-start.17
  219.9 29.6 %copy-start.26 = (f32[1,2]{1,0:T(1,128)S(1)}, f32[1,2]{1,0:T(1,128)}, u32[]{:S(2)}) copy-start(f32[1,2]{1,0:T(1,128)} %param.9) | copy-start | bytes 28
Sparse Core Ops, SparseCore 0:
  256.5 57.7 reduce-scatter.1
